TPU v7x, 512 devices: a whole 4x4x16 slice. The times are simulated.
512 devices in a mesh: section: 16 (over y, z_hi), dp: 8 (over x, core), mp: 4 (over z_lo).
Axes of the slice: x: 4, y: 4, z: 16 (z_hi: 4, z_lo: 4; z = z_hi * 4 + z_lo), core: 2. Of those that a mesh axis runs over, the one named last changes fastest.
Arguments:
- act_in: bfloat16 [16, 160, 6144], P('section', None, ('dp', 'mp')), may hold values from -6 to 6
- grad_in: bfloat16 [16, 160, 6144], P('section', None, ('dp', 'mp')), may hold values from -6 to 6
- weight: bfloat16 [16, 6144, 6144], P('section', ('dp', 'mp')), may hold values from -0.078125 to 0.078125
- gain: bfloat16 [16, 6144], P('section', ('dp', 'mp')), may hold values from 0.5 to 1.5
- preempted: int32 [16, 160], P('section'), may hold values 0 or 1
Outputs:
- next_input: bfloat16 [16, 160, 6144], P('section', None, ('dp', 'mp'))
- shadow: bfloat16 [16, 160, 6144], P('section', None, ('dp', 'mp'))
- input_grad: bfloat16 [16, 160, 6144], P('section', None, ('dp', 'mp'))
- weight_grad: bfloat16 [16, 6144, 6144], P('section', ('dp', 'mp'))
- gain_grad: float32 [16, 6144], P('section', ('dp', 'mp'))
All inputs are finite; a program needn't handle non-finite values. No bound on the sum of `preempted` on one device may be relied on, other than what follows from the above.
Results may differ from a plain program's by a relative error of at most 0.0062.
Values may be sent and summed in bfloat16 or wider, within the bound.
A program may use at most 64 MiB of HBM per device.

v0:
```python
import jax
import jax.numpy as jnp
from jax import lax
from jax.sharding import PartitionSpec as P

EPS = 1e-05


def passed_along(value, axis, steps):
    count = lax.axis_size(axis)
    initial, last = (max(0, -steps), min(count, count - steps))
    return lax.ppermute(value, axis, [(source, source + steps) for source in range(initial, last)])


def row_totals(pieces):
    return lax.psum((pieces[0], pieces[1]), ("dp", "mp"))


def layer_forward(tokens, weights, gain_row, features):
    widened = tokens.astype(jnp.float32)
    totals = row_totals((jnp.sum(widened, -1), jnp.sum(widened * widened, -1)))
    row_mean = totals[0] / features
    variance = totals[1] / features - row_mean * row_mean
    inv_std = lax.rsqrt(variance + EPS)
    x_hat = (widened - row_mean[:, None]) * inv_std[:, None]
    normed = (x_hat * gain_row.astype(jnp.float32)).astype(jnp.bfloat16)
    gathered = lax.all_gather(normed, ("dp", "mp"), axis=1, tiled=True)
    preact = lax.dot_general(
        gathered, weights, (((1,), (1,)), ((), ())), preferred_element_type=jnp.float32
    )
    layer_out = (widened + jax.nn.gelu(preact)).astype(jnp.bfloat16)
    return (layer_out, preact, gathered, x_hat, inv_std)


def shards(act_in, grad_in, weight, gain, preempted):
    tokens = act_in[0]
    weights = weight[0]
    gain_row = gain[0]
    features = float(weights.shape[1])
    layer_out, preact, gathered, x_hat, inv_std = layer_forward(tokens, weights, gain_row, features)
    section_index = lax.axis_index("section")
    section_count = lax.axis_size("section")
    active = (preempted[0] * (section_index < section_count - 1).astype(jnp.int32)).astype(
        jnp.float32
    )
    arrived = passed_along(layer_out, "section", 1)
    next_weights, next_gain = passed_along((weights, gain_row), "section", -1)
    redundant = layer_forward(layer_out, next_weights, next_gain, features)[0]
    shadow = (redundant.astype(jnp.float32) * active[:, None]).astype(jnp.bfloat16)
    cotangent = grad_in[0].astype(jnp.float32)
    _, pullback = jax.vjp(jax.nn.gelu, preact)
    dpre = pullback(cotangent)[0].astype(jnp.bfloat16)
    weight_grad = lax.dot_general(
        dpre, gathered, (((0,), (0,)), ((), ())), preferred_element_type=jnp.float32
    ).astype(jnp.bfloat16)
    dnormed = lax.psum_scatter(
        lax.dot_general(
            weights, dpre, (((0,), (1,)), ((), ())), preferred_element_type=jnp.float32
        ),
        ("dp", "mp"),
        scatter_dimension=0,
        tiled=True,
    ).T
    gain_grad = jnp.sum(dnormed * x_hat, 0)
    dhat = dnormed * gain_row.astype(jnp.float32)
    totals = row_totals((jnp.sum(dhat, -1), jnp.sum(dhat * x_hat, -1)))
    mean_grad = totals[0] / features
    mean_proj = totals[1] / features
    dinput = inv_std[:, None] * (dhat - mean_grad[:, None] - x_hat * mean_proj[:, None])
    input_grad = (cotangent + dinput).astype(jnp.bfloat16)
    return (arrived[None], shadow[None], input_grad[None], weight_grad[None], gain_grad[None])


def solution(mesh):
    return jax.shard_map(
        shards,
        mesh=mesh,
        in_specs=(
            P("section", None, ("dp", "mp")),
            P("section", None, ("dp", "mp")),
            P("section", ("dp", "mp"), None),
            P("section", ("dp", "mp")),
            P("section", None),
        ),
        out_specs=(
            P("section", None, ("dp", "mp")),
            P("section", None, ("dp", "mp")),
            P("section", None, ("dp", "mp")),
            P("section", ("dp", "mp"), None),
            P("section", ("dp", "mp")),
        ),
        check_vma=False,
    )
```

profile of v0, /device:TPU:1, one launch (start us, length us, event | category | flops | bytes accessed | tf_op | source)
XLA Modules:
  0.0 700.8 jit_solution(17975544396967250677)
XLA Ops:
  7.2 0.0 all-gather.5.cloned.1.call-start
  7.2 1.0 convert_reduce_fusion.1
  8.2 1.0 fusion.14
  9.2 0.7 reduce.1
  9.9 69.5 %all-reduce.1 = (f32[160]{0:T(256)S(1)}, f32[160]{0:T(256)S(1)}) all-reduce(f32[160]{0:T(256)S(1)} %fusion.14, f32[160]{0:T(256)S(1)} %convert_reduce_fusion.1), channel_id=1, replica_groups=mesh['section'=16,'dp'=8,'mp'=4] {'dp','mp'}, use_global_device_ids=true, to_apply=%region_3.0 | all-reduce | flops 320 | bytes 2560 | tf_op jit(solution)/shard_map/psum | solution.py:16
  79.5 1.6 fusion.43
  81.1 0.0 all-gather.5.cloned.1.call-update
  81.1 0.0 reduce-scatter.4.cloned.1.call-start
  81.2 97.7 %all-gather.5.cloned.1.call-done = bf16[32,192,160]{1,2,0:T(8,128)(2,1)} async-done(((bf16[1,192,160]{1,2,0:T(8,128)(2,1)}), bf16[32,192,160]{1,2,0:T(8,128)(2,1)}) %all-gather.5.cloned.1.call-update) | async-done | bytes 1966096 | tf_op jit(solution)/shard_map/all_gather | solution.py:27
  178.9 4.7 copy.12
  183.7 4.6 reshape.31
  188.3 0.0 copy-start
  188.3 0.0 copy-start.2
  188.3 2.7 fusion.45
  191.0 0.0 copy-done
  191.0 0.0 copy-done.2
  191.0 2.7 convolution_bitcast_fusion
  193.7 6.0 copy.14
  199.7 0.0 copy-start.1
  199.7 0.0 copy-start.3
  199.7 0.0 reduce-scatter.4.cloned.1.call-update
  199.8 0.0 all-gather.7.cloned.1.call-start
  199.8 1.3 collective-permute-start.1
  201.1 7.0 collective-permute-done.1
  208.1 160.6 %reduce-scatter.4.cloned.1.call-done = f32[192,160]{1,0:T(8,128)} async-done(((f32[6144,160]{1,0:T(8,128)}), f32[192,160]{1,0:T(8,128)}) %reduce-scatter.4.cloned.1.call-update) | async-done | bytes 122896
  368.7 1.0 copy.15
  369.7 0.0 copy-done.1
  369.8 0.8 fusion.13
  370.6 71.5 %all-reduce = (f32[160]{0:T(256)S(1)}, f32[160]{0:T(256)S(1)}, f32[160]{0:T(256)S(1)}, f32[160]{0:T(256)S(1)}) all-reduce(f32[160]{0:T(256)S(1)} %get-tuple-element.17, f32[160]{0:T(256)S(1)} %get-tuple-element.18, f32[160]{0:T(256)S(1)} %get-tuple-element.6, ...), channel_id=1, replica_groups=mesh['section'=16,'dp'=8,'mp'=4] {'dp','mp'}, use_global_device_ids=true, to_apply=%region_7.0 | all-reduce | flops 640 | bytes 5120 | tf_op jit(solution)/shard_map/psum | solution.py:16
  442.1 0.8 fusion.41
  442.8 0.0 all-gather.7.cloned.1.call-update
  442.9 1.3 collective-permute-start.2
  444.2 0.0 copy-done.3
  444.2 2.3 fusion
  446.5 7.9 %collective-permute-start = (bf16[160,192]{1,0:T(8,128)(2,1)S(1)}, bf16[160,192]{1,0:T(8,128)(2,1)S(1)}, u32[]{:S(2)}, u32[]{:S(2)}) collective-permute-start(bf16[160,192]{1,0:T(8,128)(2,1)S(1)} %get-tuple-element.19), channel_id=1, source_target_pairs={{0,32},{32,64},{64,96},{96,128},{128,160},{160,192},{192,224},{224... | collective-permute-start | bytes 184328 | tf_op jit(solution)/shard_map/ppermute | solution.py:12
  454.4 0.8 fusion.42
  455.2 1.0 collective-permute-done
  456.2 226.6 %all-gather.7.cloned.1.call-done = bf16[32,192,160]{1,2,0:T(8,128)(2,1)} async-done(((bf16[1,192,160]{1,2,0:T(8,128)(2,1)}), bf16[32,192,160]{1,2,0:T(8,128)(2,1)}) %all-gather.7.cloned.1.call-update) | async-done | bytes 1966096 | tf_op jit(solution)/shard_map/all_gather | solution.py:27
  682.8 3.2 copy.13
  686.0 3.8 reshape.33
  689.8 0.0 collective-permute-done.2
  689.8 3.9 fusion.40
  693.6 0.6 copy.17
  (6 shorter events, 0.0 us)
Async XLA Ops:
  7.2 171.8 %all-gather.5.cloned.1.call-start = ((), (), s32[]{:S(2)}) async-start(), calls=%async_computation.1 | async-start | bytes 2703360 | tf_op jit(solution)/shard_map/all_gather | solution.py:27
  81.1 287.6 %reduce-scatter.4.cloned.1.call-start = ((), (), s32[]{:S(2)}) async-start(), calls=%async_computation.3 | async-start | bytes 6488064
  188.3 2.7 copy-start
  188.3 2.7 copy-start.2
  199.7 170.0 %copy-start.1 = (bf16[1,160,192]{2,1,0:T(8,128)(2,1)S(1)}, bf16[1,160,192]{2,1,0:T(8,128)(2,1)}, u32[]{:S(2)}) copy-start(bf16[1,160,192]{2,1,0:T(8,128)(2,1)} %param.5) | copy-start | bytes 184324
  199.7 244.5 %copy-start.3 = (s32[1,160]{1,0:T(1,128)S(1)}, s32[1,160]{1,0:T(1,128)}, u32[]{:S(2)}) copy-start(s32[1,160]{1,0:T(1,128)} %param.9) | copy-start | bytes 1924
  199.8 483.0 %all-gather.7.cloned.1.call-start = ((), (), s32[]{:S(2)}) async-start(), calls=%async_computation.2 | async-start | bytes 2703360 | tf_op jit(solution)/shard_map/all_gather | solution.py:27
  199.8 8.3 %collective-permute-start.1 = (bf16[192]{0:T(256)(128)(2,1)S(1)}, bf16[192]{0:T(256)(128)(2,1)S(1)}, u32[]{:S(2)}, u32[]{:S(2)}) collective-permute-start(bf16[192]{0:T(256)(128)(2,1)S(1)} %reduce.1), channel_id=1, source_target_pairs={{32,0},{64,32},{96,64},{128,96},{160,128},{192,160},{224,192},{256... | collective-permute-start | bytes 1160 | tf_op jit(solution)/shard_map/ppermute | solution.py:12
  442.9 246.9 %collective-permute-start.2 = (bf16[192,6144]{1,0:T(8,128)(2,1)}, bf16[192,6144]{1,0:T(8,128)(2,1)}, u32[]{:S(2)}, u32[]{:S(2)}) collective-permute-start(bf16[192,6144]{1,0:T(8,128)(2,1)} %bitcast.91), channel_id=1, source_target_pairs={{32,0},{64,32},{96,64},{128,96},{160,128},{192,160},{224,192},{256... | collective-permute-start | bytes 7077896 | tf_op jit(solution)/shard_map/ppermute | solution.py:12
  446.5 9.7 %collective-permute-start = (bf16[160,192]{1,0:T(8,128)(2,1)S(1)}, bf16[160,192]{1,0:T(8,128)(2,1)S(1)}, u32[]{:S(2)}, u32[]{:S(2)}) collective-permute-start(bf16[160,192]{1,0:T(8,128)(2,1)S(1)} %get-tuple-element.19), channel_id=1, source_target_pairs={{0,32},{32,64},{64,96},{96,128},{128,160},{160,192},{192,224},{224... | collective-permute-start | bytes 184328 | tf_op jit(solution)/shard_map/ppermute | solution.py:12
Sparse Core Ops, SparseCore 0:
  81.3 97.6 all-gather.4
  199.9 168.7 reduce-scatter.3
  443.0 239.7 all-gather.6
where the time goes:
time: 714 us; the launch traced here: 701 us
  waiting for transfers between devices  493 us (69%)
  blocking collectives  141 us (20%)
  local copies, waits for them, and re-layouts  24 us (3%)
  between operations  13.9 us (2%)
  matrix products  11.6 us (2%)
  starting transfers between devices  10.6 us (1%)
    all_gather x2, waiting for transfers between devices, layer_forward(): gathered = lax.all_gather(normed, ('dp', 'mp'), axis=1, tiled=True)  324 us
    unnamed x4, waiting for transfers between devices  161 us
    psum x2, blocking collectives, row_totals(): return lax.psum((pieces[0], pieces[1]), ('dp', 'mp'))  141 us
    unnamed x13, local copies, waits for them, and re-layouts  16.1 us
  transfers between devices with their start and end apart: 6, of which 5 were waited for; matrix products, arithmetic and copies ran while one was open for 1% of the time, Pallas kernels for 0%

commit v1 on v0

v1 whole, which is shorter than its diff:
```python
import functools

import jax
import jax.numpy as jnp
from jax import lax
from jax.experimental import pallas as pl
from jax.experimental.pallas import tpu as pltpu
from jax.sharding import PartitionSpec as P

EPS = 1e-05
MESH = pl.DeviceIdType.MESH
F32 = jnp.float32
BF16 = jnp.bfloat16
LANES = 128
HALF = 64
PAD = 16

NT = (((1,), (1,)), ((), ()))
NN = (((1,), (0,)), ((), ()))


def dot(a, b, dims):
    return lax.dot_general(a, b, dims, preferred_element_type=F32)


def low_lanes(rows):
    return lax.broadcasted_iota(jnp.int32, (rows, LANES), 1) < HALF


def half_turn(value):
    return pltpu.roll(value, HALF, 1)


def split_tiles(value):
    tail = value[:, LANES:]
    return value[:, :LANES], jnp.concatenate([tail, tail], axis=1)


def main_and_rest(value, odd):
    first, tail = split_tiles(value)
    low = low_lanes(value.shape[0])
    turned = half_turn(first)
    main = jnp.where(odd, jnp.where(low, turned, tail), first)
    rest = jnp.where(odd, jnp.where(low, first, turned), tail)
    return main, rest


def pack(value, odd):
    half = value.shape[0] // 2
    main, rest = main_and_rest(value, odd)
    here = low_lanes(half) != odd
    return main, jnp.where(here, rest[:half], rest[half:])


def unpack(main, folded, odd):
    half = folded.shape[0]
    here = low_lanes(half) != odd
    turned = half_turn(folded)
    rest = jnp.concatenate([jnp.where(here, folded, turned), jnp.where(here, turned, folded)], axis=0)
    main_turned = half_turn(main)
    first = jnp.where(odd, jnp.where(low_lanes(main.shape[0]), rest, main_turned), main)
    tail = jnp.where(odd, main_turned, rest)
    return jnp.concatenate([first, tail[:, :HALF]], axis=1)


def gelu_parts(p):
    k = 0.7978845608028654
    t = jnp.tanh(k * (p + 0.044715 * (p * p * p)))
    return t, k * (1.0 + (3.0 * 0.044715) * (p * p))


def eye(rows, columns):
    return lax.broadcasted_iota(jnp.int32, (rows, columns), 0) == lax.broadcasted_iota(
        jnp.int32, (rows, columns), 1
    )


def as_column(row):
    n = row.shape[1]
    return jnp.sum(jnp.where(eye(n, n), jnp.broadcast_to(row, (n, n)), 0.0), axis=1, keepdims=True)


def as_row(column, width):
    n = column.shape[0]
    return jnp.sum(jnp.where(eye(n, width), jnp.broadcast_to(column, (n, width)), 0.0), axis=0, keepdims=True)


COPIES = (
    [(tag, kind, k) for tag in "ab" for kind in "z+-f" for k in range(4) if (kind, k) != ("z", 0)]
    + [(tag, "s", j) for tag in "ab" for j in range(7)]
    + [("next",), ("back",)]
    + [("S", "z", k) for k in (1, 2, 3)]
    + [("S", "x", k) for k in (1, 2, 3)]
    + [("S", "c")]
    + [("C", j) for j in range(4)]
    + [("F", j) for j in range(2)]
    + [("G", j, part) for j in range(2) for part in range(2)]
    + [("Z", k) for k in (1, 2, 3)]
)
COPY_ID = {name: index for index, name in enumerate(COPIES)}


def kernel(
    sections,
    features,
    act,
    grad,
    gain,
    preempted,
    weight,
    next_out,
    shadow_out,
    input_grad_out,
    gain_grad_out,
    weight_grad_out,
    wv,
    wp,
    xs,
    xs2,
    gains,
    got1,
    got2,
    acc,
    squares,
    outgoing,
    returned,
    partial,
    from_sib,
    hop,
    g_in,
    h_out,
    z_in,
    s_own,
    s_z,
    s_x,
    s_xr,
    s_c,
    s_cr,
    mean_s,
    inv_s,
    dpre_s,
    dpre_t,
    stage,
    send_sem,
    recv_sem,
    w_sem,
    out_sem,
):
    T, F = act.shape[1], act.shape[2]
    H = T // 2
    R = T + H
    C = 4 * F
    section, dp, z = lax.axis_index("section"), lax.axis_index("dp"), lax.axis_index("mp")
    core = dp % 2
    sib = dp + 1 - 2 * core
    odd = (z % 2) == 1

    def near(c, step):
        return (c + 2 * step + 8) % 8

    up, down, far = near(dp, 1), near(dp, -1), near(dp, 2)
    to_up, to_down, to_far, to_sib = {"dp": up}, {"dp": down}, {"dp": far}, {"dp": sib}
    to_next = {"section": (section + 1) % sections}
    to_back = {"section": (section + sections - 1) % sections}

    def to_z(k):
        return {"mp": (z + k) % 4}

    def zk(k):
        return (z + 4 - k) % 4

    def rc(name, src, dst, device):
        n = COPY_ID[name]
        return pltpu.make_async_remote_copy(
            src_ref=src,
            dst_ref=dst,
            send_sem=send_sem.at[n],
            recv_sem=recv_sem.at[n],
            device_id=device,
            device_id_type=MESH,
        )

    def send(name, src, dst, device):
        rc(name, src, dst, device).start()

    def arrive(name, dst):
        rc(name, dst, dst, to_sib).wait_recv()

    def sent(name, src):
        rc(name, src, src, to_sib).wait_send()

    def weight_copy(c):
        return pltpu.make_async_copy(
            weight.at[0, :, pl.ds(c * C, C)], wv.at[c], w_sem.at[c]
        )

    for c in range(8):
        weight_copy(c).start()
    barrier = pltpu.get_barrier_semaphore()
    partners = [to_z(1), to_z(2), to_z(3), to_up, to_down, to_far, to_sib, to_next, to_back]
    for device in partners:
        pl.semaphore_signal(barrier, inc=1, device_id=device, device_id_type=MESH)

    x_own = act[0].astype(F32)
    main, folded = pack(x_own, odd)
    got1[dp, z, :T] = main.astype(BF16)
    got1[dp, z, T:R] = folded.astype(BF16)
    gain_row = gain[...].astype(F32)
    g_main, g_rest = main_and_rest(jnp.broadcast_to(gain_row, (PAD, F)), odd)
    first_row = lax.broadcasted_iota(jnp.int32, (PAD, LANES), 0) == 0
    got1[dp, z, R:] = jnp.where(first_row, g_main, g_rest).astype(BF16)
    pl.semaphore_wait(barrier, len(partners))

    def gather_begin(tag, got):
        own = got.at[dp, z]
        for k in (1, 2, 3):
            send((tag, "z", k), own, own, to_z(k))
        send((tag, "+", 0), own, own, to_up)
        send((tag, "-", 0), own, own, to_down)

    gather_begin("a", got1)

    ones = jnp.ones((PAD, C), BF16)

    def fill(c, carry):
        xs[c, T:] = ones
        wp[c, F:] = ones
        return carry

    lax.fori_loop(0, 8, fill, 0)
    xs2[T:] = ones

    def chunk_of(i):
        step = jnp.where(i < 2, 0, jnp.where(i > 5, 2, jnp.where(i % 2 == 0, 3, 1)))
        flip = jnp.where((i == 1) | (i == 4) | (i == 5) | (i == 7), 1, 0)
        mine = (dp + 2 * step) % 8
        return mine + flip * (1 - 2 * core)

    def gather_step(tag, got, i):
        other_up, other_down, other_far = near(sib, 1), near(sib, -1), near(sib, 2)

        @pl.when(i == 0)
        def _():
            for k in (1, 2, 3):
                block = got.at[dp, zk(k)]
                arrive((tag, "z", k), block)
                send((tag, "+", k), block, block, to_up)
                send((tag, "-", k), block, block, to_down)
            send((tag, "s", 0), got.at[dp], got.at[dp], to_sib)

        @pl.when(i == 1)
        def _():
            for k in (0, 1):
                a, b = got.at[down, zk(k)], got.at[up, zk(k)]
                arrive((tag, "+", k), a)
                arrive((tag, "-", k), b)
                if k % 2 == 0:
                    send((tag, "f", k), a, a, to_up)
                else:
                    send((tag, "f", k), b, b, to_down)
            arrive((tag, "s", 0), got.at[sib])

        @pl.when(i == 2)
        def _():
            for k in (2, 3):
                a, b = got.at[down, zk(k)], got.at[up, zk(k)]
                arrive((tag, "+", k), a)
                arrive((tag, "-", k), b)
                if k % 2 == 0:
                    send((tag, "f", k), a, a, to_up)
                else:
                    send((tag, "f", k), b, b, to_down)
            send((tag, "s", 1), got.at[down], got.at[down], to_sib)
            send((tag, "s", 2), got.at[up], got.at[up], to_sib)

        @pl.when(i == 4)
        def _():
            arrive((tag, "s", 1), got.at[other_down])

        @pl.when(i == 5)
        def _():
            arrive((tag, "s", 2), got.at[other_up])

        @pl.when(i == 6)
        def _():
            for k in range(4):
                block = got.at[far, zk(k)]
                arrive((tag, "f", k), block)
                send((tag, "s", 3 + k), block, block, to_sib)

        @pl.when(i == 7)
        def _():
            for k in range(4):
                arrive((tag, "s", 3 + k), got.at[other_far, zk(k)])

    def gather_end(tag, got):
        for k in range(4):
            if k:
                sent((tag, "z", k), got.at[0, 0])
            for kind in "+-f":
                sent((tag, kind, k), got.at[0, 0])
            sent((tag, "s", 3 + k), got.at[0, 0])
        for j in range(3):
            sent((tag, "s", j), got.at[0])

    low = low_lanes(H)

    def unfold_chunk(got, c, keep):
        total = squares[...]
        for p in range(2):
            r0 = got[c, 2 * p, T:R].astype(F32)
            r1 = got[c, 2 * p + 1, T:R].astype(F32)
            middle = jnp.concatenate([jnp.where(low, r0, r1), half_turn(jnp.where(low, r1, r0))], axis=0)
            t0 = got[c, 2 * p, :T]
            t2 = got[c, 2 * p + 1, :T]
            keep(3 * p, t0)
            keep(3 * p + 1, middle.astype(BF16))
            keep(3 * p + 2, t2)
            t0, t2 = t0.astype(F32), t2.astype(F32)
            total = total + (t0 * t0 + middle * middle + t2 * t2)
        squares[...] = total

    acc[...] = jnp.zeros_like(acc)
    squares[...] = jnp.zeros_like(squares)
    for c in range(8):
        weight_copy(c).wait()

    def first_layer(i, carry):
        gather_step("a", got1, i)
        c = chunk_of(i)
        row_low = low_lanes(1)
        for p in range(2):
            g0 = got1[c, 2 * p, R:].astype(F32)
            g1 = got1[c, 2 * p + 1, R:].astype(F32)
            for j, row in enumerate((g0[0:1], jnp.where(row_low, g0[1:2], g1[1:2]), g1[0:1])):
                gains[c, :, (3 * p + j) * LANES : (3 * p + j + 1) * LANES] = jnp.broadcast_to(row, (8, LANES))
        wp[c, :F] = (wv[c].astype(F32) * gains[c, 0:1]).astype(BF16)

        def keep(t, value):
            xs[c, :T, t * LANES : (t + 1) * LANES] = value

        unfold_chunk(got1, c, keep)
        acc[...] += dot(xs[c], wp[c], NT)
        return carry

    lax.fori_loop(0, 8, first_layer, 0)

    def row_statistics():
        mean = acc[:T, F : F + 1] / features
        variance = jnp.sum(squares[...], axis=1, keepdims=True) / features - mean * mean
        return mean, lax.rsqrt(variance + EPS)

    mean, inv_std = row_statistics()
    weight_sums = acc[T : T + 1, :F]
    preact = inv_std * (acc[:T, :F] - mean * weight_sums)
    t, slope = gelu_parts(preact)
    layer_out = x_own + 0.5 * preact * (1.0 + t)
    main, folded = pack(layer_out.astype(BF16).astype(F32), odd)
    outgoing[:T] = main.astype(BF16)
    outgoing[T:] = folded.astype(BF16)
    send(("next",), outgoing, got2.at[dp, z], to_next)

    derivative = 0.5 * (1.0 + t) + 0.5 * preact * (1.0 - t * t) * slope
    dpre = (grad[0].astype(F32) * derivative).astype(BF16)
    dpre_s[...] = dpre
    dpre_f = dpre.astype(F32)
    mean_s[...] = jnp.broadcast_to(mean, (T, LANES))
    inv_s[...] = jnp.broadcast_to(inv_std, (T, LANES))
    sum_grad = jnp.sum(dpre_f * weight_sums, axis=1, keepdims=True)
    sum_proj = jnp.sum(dpre_f * preact, axis=1, keepdims=True)
    width = s_own.shape[1]
    row_is_0 = lax.broadcasted_iota(jnp.int32, (8, width), 0) == 0
    s_own[...] = jnp.where(row_is_0, as_row(sum_grad, width), as_row(sum_proj, width))
    for k in (1, 2, 3):
        send(("S", "z", k), s_own, s_z.at[k - 1], to_z(k))
    dpre_t[...] = dot(jnp.where(eye(F, F), 1.0, 0.0).astype(BF16), dpre, NT).astype(BF16)

    def partial_chunk(c):
        product = dot(dpre_s[...], wv[c], NN)
        for p in range(2):
            tile = [product[:, (3 * p + j) * LANES : (3 * p + j + 1) * LANES] for j in range(3)]
            top, bottom = tile[1][:H], half_turn(tile[1][H:])
            partial[c, 2 * p, :T] = tile[0].astype(BF16)
            partial[c, 2 * p, T:] = jnp.where(low, top, bottom).astype(BF16)
            partial[c, 2 * p + 1, :T] = tile[2].astype(BF16)
            partial[c, 2 * p + 1, T:] = jnp.where(low, bottom, top).astype(BF16)

    def x_of(j):
        return (dp // 2 + jnp.where(j == 0, 2, jnp.where(j == 1, 1, jnp.where(j == 2, 3, 0)))) % 4

    def partial_step(i, carry):
        j = i % 4
        theirs = i < 4
        x = x_of(j)
        c = 2 * x + jnp.where(theirs, 1 - core, core)
        partial_chunk(c)
        for n in range(4):

            @pl.when(i == n)
            def _():
                send(("C", n), partial.at[c], from_sib.at[x], to_sib)

        return carry

    lax.fori_loop(0, 8, partial_step, 0)

    def fold_in(c, source, index, first=0, count=4):
        for b in range(first, first + count):
            partial[c, b] = (partial[c, b].astype(F32) + source[index, b - first].astype(F32)).astype(BF16)

    def weight_grad_copy(c):
        return pltpu.make_async_copy(
            stage.at[c], weight_grad_out.at[0, :, pl.ds(pl.multiple_of(c * C, C), C)], out_sem.at[c]
        )

    def weight_grad_chunk(c):
        x = xs[c, :T].astype(F32)
        normed = ((x - mean_s[:, 0:1]) * inv_s[:, 0:1] * gains[c, 0:1]).astype(BF16)
        stage[c] = dot(dpre_t[...], normed, NN).astype(BF16)
        weight_grad_copy(c).start()

    arrive(("next",), got2.at[dp, z])
    gather_begin("b", got2)

    def from_sibling(n):
        x = x_of(n)
        arrive(("C", n), from_sib.at[x])
        fold_in(2 * x + core, from_sib, x)

    def second_layer(i, carry):
        gather_step("b", got2, i)

        @pl.when(i == 1)
        def _():
            from_sibling(0)
            send(("F", 0), partial.at[far, 0:2], hop.at[0], to_up)
            send(("F", 1), partial.at[far, 2:4], hop.at[1], to_down)
            for n in (1, 2, 3):
                from_sibling(n)
            send(("G", 0, 0), partial.at[up, 2:4], g_in.at[0, 2:4], to_up)
            send(("G", 1, 0), partial.at[down, 0:2], g_in.at[1, 0:2], to_down)

        @pl.when(i == 2)
        def _():
            for k in (1, 2, 3):
                arrive(("S", "z", k), s_z.at[k - 1])
            s_x[...] = s_own[...] + (s_z[0] + s_z[1] + s_z[2])
            for k in (1, 2, 3):
                send(("S", "x", k), s_x, s_xr.at[k - 1], {"dp": near(dp, k)})

        @pl.when(i == 4)
        def _():
            arrive(("F", 0), hop.at[0])
            fold_in(up, hop, 0, 0, 2)
            send(("G", 0, 1), partial.at[up, 0:2], g_in.at[0, 0:2], to_up)
            arrive(("F", 1), hop.at[1])
            fold_in(down, hop, 1, 2, 2)
            send(("G", 1, 1), partial.at[down, 2:4], g_in.at[1, 2:4], to_down)

        @pl.when(i == 5)
        def _():
            for k in (1, 2, 3):
                arrive(("S", "x", k), s_xr.at[k - 1])
            s_c[...] = s_x[...] + (s_xr[0] + s_xr[1] + s_xr[2])
            send(("S", "c"), s_c, s_cr, to_sib)

        weight_grad_chunk(i)
        c = chunk_of(i)

        def keep(t, value):
            xs2[:T, t * LANES : (t + 1) * LANES] = value

        unfold_chunk(got2, c, keep)
        acc[...] += dot(xs2[...], wp[c], NT)
        return carry

    acc[...] = jnp.zeros_like(acc)
    squares[...] = jnp.zeros_like(squares)
    lax.fori_loop(0, 8, second_layer, 0)

    mean2, inv_std2 = row_statistics()
    preact2 = inv_std2 * (acc[:T, :F] - mean2 * acc[T : T + 1, :F])
    t2, _ = gelu_parts(preact2)
    x_next = unpack(got2[dp, z, :T].astype(F32), got2[dp, z, T:].astype(F32), odd)
    redundant = (x_next + 0.5 * preact2 * (1.0 + t2)).astype(BF16).astype(F32)
    main, folded = pack(redundant, odd)
    sent(("next",), outgoing)
    outgoing[:T] = main.astype(BF16)
    outgoing[T:] = folded.astype(BF16)
    send(("back",), outgoing, returned, to_back)
    next_out[0] = jnp.where(section > 0, x_next, 0.0).astype(BF16)

    for j in range(2):
        for part in range(2):
            half = g_in.at[j, 0:2] if j == part ^ 1 else g_in.at[j, 2:4]
            arrive(("G", j, part), half)

    def sum_x(b):
        return partial[dp, b].astype(F32) + (g_in[0, b].astype(F32) + g_in[1, b].astype(F32))

    for k in (1, 2, 3):
        b = (z + k) % 4
        h_out[k - 1] = sum_x(b).astype(BF16)
        send(("Z", k), h_out.at[k - 1], z_in.at[k - 1], to_z(k))
    total = sum_x(z)
    for k in (1, 2, 3):
        arrive(("Z", k), z_in.at[k - 1])
        total = total + z_in[k - 1].astype(F32)
    dnormed = unpack(total[:T], total[T:], odd)

    arrive(("S", "c"), s_cr)
    sums = (s_c[...] + s_cr[...])[:, :T] / features
    mean_grad = as_column(sums[0:1])
    mean_proj = as_column(sums[1:2])
    inv_std = inv_s[:, 0:1]
    x_hat = (act[0].astype(F32) - mean_s[:, 0:1]) * inv_std
    gain_grad_out[...] = jnp.sum(dnormed * x_hat, axis=0, keepdims=True)
    dhat = dnormed * gain[...].astype(F32)
    dinput = inv_std * (dhat - mean_grad - x_hat * mean_proj)
    input_grad_out[0] = (grad[0].astype(F32) + dinput).astype(BF16)

    active = as_column(preempted[...].astype(F32)) * jnp.where(section < sections - 1, 1.0, 0.0)
    arrive(("back",), returned)
    shadow = unpack(returned[:T].astype(F32), returned[T:].astype(F32), odd)
    shadow_out[0] = (shadow * active).astype(BF16)

    gather_end("a", got1)
    gather_end("b", got2)
    sent(("back",), outgoing)
    for k in (1, 2, 3):
        sent(("S", "z", k), s_own)
        sent(("S", "x", k), s_x)
        sent(("Z", k), h_out.at[k - 1])
    sent(("S", "c"), s_c)
    for n in range(4):
        sent(("C", n), partial.at[0])
    for j in range(2):
        sent(("F", j), hop.at[0])
        for part in range(2):
            sent(("G", j, part), hop.at[0])
    for c in range(8):
        weight_grad_copy(c).wait()


def shards(sections, devices, act_in, grad_in, weight, gain, preempted):
    _, T, F = act_in.shape
    D = weight.shape[2]
    R = T + T // 2
    C = 4 * F
    vmem, anywhere = pl.BlockSpec(memory_space=pltpu.VMEM), pl.BlockSpec(memory_space=pl.ANY)
    shape = jax.ShapeDtypeStruct
    copies = len(COPIES)
    results = pl.pallas_call(
        functools.partial(kernel, sections, float(D)),
        out_shape=(
            shape((1, T, F), BF16),
            shape((1, T, F), BF16),
            shape((1, T, F), BF16),
            shape((1, F), F32),
            shape((1, F, D), BF16),
        ),
        in_specs=[vmem, vmem, vmem, vmem, anywhere],
        out_specs=(vmem, vmem, vmem, vmem, anywhere),
        scratch_shapes=[
            pltpu.VMEM((8, F, C), BF16),
            pltpu.VMEM((8, F + PAD, C), BF16),
            pltpu.VMEM((8, T + PAD, C), BF16),
            pltpu.VMEM((T + PAD, C), BF16),
            pltpu.VMEM((8, 8, C), F32),
            pltpu.VMEM((8, 4, R + PAD, LANES), BF16),
            pltpu.VMEM((8, 4, R, LANES), BF16),
            pltpu.VMEM((T + PAD, F + PAD), F32),
            pltpu.VMEM((T, LANES), F32),
            pltpu.VMEM((R, LANES), BF16),
            pltpu.VMEM((R, LANES), BF16),
            pltpu.VMEM((8, 4, R, LANES), BF16),
            pltpu.VMEM((4, 4, R, LANES), BF16),
            pltpu.VMEM((2, 2, R, LANES), BF16),
            pltpu.VMEM((2, 4, R, LANES), BF16),
            pltpu.VMEM((3, R, LANES), BF16),
            pltpu.VMEM((3, R, LANES), BF16),
            pltpu.VMEM((8, 256), F32),
            pltpu.VMEM((3, 8, 256), F32),
            pltpu.VMEM((8, 256), F32),
            pltpu.VMEM((3, 8, 256), F32),
            pltpu.VMEM((8, 256), F32),
            pltpu.VMEM((8, 256), F32),
            pltpu.VMEM((T, LANES), F32),
            pltpu.VMEM((T, LANES), F32),
            pltpu.VMEM((T, F), BF16),
            pltpu.VMEM((F, T), BF16),
            pltpu.VMEM((8, F, C), BF16),
            pltpu.SemaphoreType.DMA((copies,)),
            pltpu.SemaphoreType.DMA((copies,)),
            pltpu.SemaphoreType.DMA((8,)),
            pltpu.SemaphoreType.DMA((8,)),
        ],
        compiler_params=pltpu.CompilerParams(
            collective_id=0, has_side_effects=True, vmem_limit_bytes=40 * 1024 * 1024
        ),
    )(act_in, grad_in, gain, preempted, weight)
    next_input, shadow, input_grad, gain_grad, weight_grad = results
    return next_input, shadow, input_grad, weight_grad, gain_grad


def solution(mesh):
    return jax.shard_map(
        functools.partial(shards, mesh.shape["section"], mesh.shape["dp"] * mesh.shape["mp"]),
        mesh=mesh,
        in_specs=(
            P("section", None, ("dp", "mp")),
            P("section", None, ("dp", "mp")),
            P("section", ("dp", "mp"), None),
            P("section", ("dp", "mp")),
            P("section", None),
        ),
        out_specs=(
            P("section", None, ("dp", "mp")),
            P("section", None, ("dp", "mp")),
            P("section", None, ("dp", "mp")),
            P("section", ("dp", "mp"), None),
            P("section", ("dp", "mp")),
        ),
        check_vma=False,
    )
```

time: 714 us -> 88.5 us (0.12); the launches traced: 701 us -> 88.2 us
  waiting for transfers between devices: 493 us -> 0 us
  blocking collectives: 141 us -> 0 us
  Pallas kernels: 0 us -> 78.9 us
  local copies, waits for them, and re-layouts: 24 us -> 8.66 us
  between operations: 13.9 us -> 0.66 us
  matrix products: 11.6 us -> 0 us
  starting transfers between devices: 10.6 us -> 0 us
    all_gather x2 -> x0, waiting for transfers between devices: 324 us -> none  [layer_forward(): gathered = lax.all_gather(normed, ('dp', 'mp'), axis=1, tiled=True)]
    unnamed x4 -> x0, waiting for transfers between devices: 161 us -> none
    psum x2 -> x0, blocking collectives: 141 us -> none  [row_totals(): return lax.psum((pieces[0], pieces[1]), ('dp', 'mp'))]
    pallas_call x0 -> x1, Pallas kernels: none -> 78.9 us  [shards(): pl.pallas_call(functools.partial(kernel, sections, float(D)), out_shape=(...]
    dot_general x4 -> x0, matrix products: 11.6 us -> none  [the longest x2 6.56 us: layer_forward(): lax.dot_general(gathered, weights, (((1,), (1,)), ((), ())), preferred_el...]
    ppermute x3 -> x0, starting transfers between devices: 10.5 us -> none  [passed_along(): lax.ppermute(value, axis, [(source, source + steps) for source in range(i...]
    ppermute x3 -> x0, waiting for transfers between devices: 8 us -> none  [passed_along(): lax.ppermute(value, axis, [(source, source + steps) for source in range(i...]
    all_gather x2 -> x0, local copies, waits for them, and re-layouts: 7.96 us -> none  [layer_forward(): gathered = lax.all_gather(normed, ('dp', 'mp'), axis=1, tiled=True)]
  transfers between devices with their start and end apart: 6 -> 0, of which waited for: 5 -> 0; matrix products, arithmetic and copies ran while one was open for 1% -> 0% of each run, Pallas kernels for 0% -> 0%
where the time goes in v1:
time: 88.5 us; the launch traced here: 88.2 us
  Pallas kernels  78.9 us (89%)
  local copies, waits for them, and re-layouts  8.66 us (10%)
    pallas_call x1, Pallas kernels, shards(): pl.pallas_call(functools.partial(kernel, sections, float(D)), out_shape=(...  78.9 us
    unnamed x15, local copies, waits for them, and re-layouts  8.66 us

profile of v1, /device:TPU:1, one launch (start us, length us, event | category | flops | bytes accessed | tf_op | source)
XLA Modules:
  0.0 88.2 jit_solution(5584195812946669966)
XLA Ops:
  0.6 0.0 copy-start
  0.6 1.7 %copy-done = bf16[1,192,6144]{2,1,0:T(8,128)(2,1)S(1)} copy-done((bf16[1,192,6144]{2,1,0:T(8,128)(2,1)S(1)}, bf16[1,192,6144]{2,1,0:T(8,128)(2,1)}, u32[]{:S(2)}) %copy-start) | copy-done | bytes 2359320
  2.3 0.0 copy-start.1
  2.3 0.9 %copy-done.1 = bf16[1,160,192]{2,1,0:T(8,128)(2,1)S(1)} copy-done((bf16[1,160,192]{2,1,0:T(8,128)(2,1)S(1)}, bf16[1,160,192]{2,1,0:T(8,128)(2,1)}, u32[]{:S(2)}) %copy-start.1) | copy-done | bytes 61464
  3.2 0.0 copy-start.2
  3.2 0.9 %copy-done.2 = bf16[1,160,192]{2,1,0:T(8,128)(2,1)S(1)} copy-done((bf16[1,160,192]{2,1,0:T(8,128)(2,1)S(1)}, bf16[1,160,192]{2,1,0:T(8,128)(2,1)}, u32[]{:S(2)}) %copy-start.2) | copy-done | bytes 61464
  4.1 0.0 copy-start.3
  4.1 0.7 copy-done.3
  4.8 0.0 copy-start.4
  4.8 0.7 copy-done.4
  5.4 78.9 %shard_map.92 = (bf16[1,160,192]{2,1,0:T(8,128)(2,1)S(1)}, bf16[1,160,192]{2,1,0:T(8,128)(2,1)S(1)}, bf16[1,160,192]{2,1,0:T(8,128)(2,1)S(1)}, f32[1,192]{1,0:T(1,128)S(1)}, bf16[1,192,6144]{2,1,0:T(8,128)(2,1)S(1)}) custom-call(bf16[1,160,192]{2,1,0:T(8,128)(2,1)S(1)} %copy-done.1, bf16[1,160,192]{2,1,0:T(8,128)(2,1)S(1)} %copy-done.2, ...), custom_call_target="tpu_custom_call" | custom-call | tf_op jit(solution)/shard_map/pallas_call | solution.py:553
  84.3 0.6 copy.15
  85.0 0.6 copy.16
  85.6 0.6 copy.17
  86.2 1.4 %copy.18 = bf16[1,192,6144]{2,1,0:T(8,128)(2,1)} copy(bf16[1,192,6144]{2,1,0:T(8,128)(2,1)S(1)} %get-tuple-element.23) | data formatting | bytes 4718592
  87.7 0.6 copy.19
Async XLA Ops:
  0.6 1.7 %copy-start = (bf16[1,192,6144]{2,1,0:T(8,128)(2,1)S(1)}, bf16[1,192,6144]{2,1,0:T(8,128)(2,1)}, u32[]{:S(2)}) copy-start(bf16[1,192,6144]{2,1,0:T(8,128)(2,1)} %weight.1) | copy-start | bytes 7077892
  2.3 0.9 %copy-start.1 = (bf16[1,160,192]{2,1,0:T(8,128)(2,1)S(1)}, bf16[1,160,192]{2,1,0:T(8,128)(2,1)}, u32[]{:S(2)}) copy-start(bf16[1,160,192]{2,1,0:T(8,128)(2,1)} %act.1) | copy-start | bytes 184324
  3.2 0.9 %copy-start.2 = (bf16[1,160,192]{2,1,0:T(8,128)(2,1)S(1)}, bf16[1,160,192]{2,1,0:T(8,128)(2,1)}, u32[]{:S(2)}) copy-start(bf16[1,160,192]{2,1,0:T(8,128)(2,1)} %grad.1) | copy-start | bytes 184324
  4.1 0.7 copy-start.3
  4.8 0.7 copy-start.4

commit v2 on v0

v2 whole, which is shorter than its diff:
```python
import functools

import jax
import jax.numpy as jnp
from jax import lax
from jax.experimental import pallas as pl
from jax.experimental.pallas import tpu as pltpu
from jax.sharding import PartitionSpec as P

EPS = 1e-05
MESH = pl.DeviceIdType.MESH
F32 = jnp.float32
BF16 = jnp.bfloat16
LANES = 128
HALF = 64
PAD = 16

NT = (((1,), (1,)), ((), ()))
NN = (((1,), (0,)), ((), ()))


def dot(a, b, dims):
    return lax.dot_general(a, b, dims, preferred_element_type=F32)


def low_lanes(rows):
    return lax.broadcasted_iota(jnp.int32, (rows, LANES), 1) < HALF


def half_turn(value):
    return pltpu.roll(value, HALF, 1)


def split_tiles(value):
    tail = value[:, LANES:]
    return value[:, :LANES], jnp.concatenate([tail, tail], axis=1)


def main_and_rest(value, odd):
    first, tail = split_tiles(value)
    low = low_lanes(value.shape[0])
    turned = half_turn(first)
    main = jnp.where(odd, jnp.where(low, turned, tail), first)
    rest = jnp.where(odd, jnp.where(low, first, turned), tail)
    return main, rest


def pack(value, odd):
    half = value.shape[0] // 2
    main, rest = main_and_rest(value, odd)
    here = low_lanes(half) != odd
    return main, jnp.where(here, rest[:half], rest[half:])


def unpack(main, folded, odd):
    half = folded.shape[0]
    here = low_lanes(half) != odd
    turned = half_turn(folded)
    rest = jnp.concatenate([jnp.where(here, folded, turned), jnp.where(here, turned, folded)], axis=0)
    main_turned = half_turn(main)
    first = jnp.where(odd, jnp.where(low_lanes(main.shape[0]), rest, main_turned), main)
    tail = jnp.where(odd, main_turned, rest)
    return jnp.concatenate([first, tail[:, :HALF]], axis=1)


def gelu_parts(p):
    k = 0.7978845608028654
    t = jnp.tanh(k * (p + 0.044715 * (p * p * p)))
    return t, k * (1.0 + (3.0 * 0.044715) * (p * p))


def eye(rows, columns):
    return lax.broadcasted_iota(jnp.int32, (rows, columns), 0) == lax.broadcasted_iota(
        jnp.int32, (rows, columns), 1
    )


def as_column(row):
    n = row.shape[1]
    return jnp.sum(jnp.where(eye(n, n), jnp.broadcast_to(row, (n, n)), 0.0), axis=1, keepdims=True)


def as_row(column, width, start):
    n = column.shape[0]
    here = lax.broadcasted_iota(jnp.int32, (n, width), 0) + start == lax.broadcasted_iota(jnp.int32, (n, width), 1)
    return jnp.sum(jnp.where(here, jnp.broadcast_to(column, (n, width)), 0.0), axis=0, keepdims=True)


GROUPS = 2
SPLIT = (96, 64)
COPIES = (
    [(tag, g, "z", k) for tag in "ab" for g in range(GROUPS) for k in (1, 2, 3)]
    + [(tag, g, kind, k) for tag in "ab" for g in range(GROUPS) for kind in "+-s" for k in range(4)]
    + [(tag, g, "f", k) for tag in "ab" for g in range(GROUPS) for k in range(4)]
    + [(name, g) for name in ("next", "back") for g in range(GROUPS)]
    + [("S", "z", k) for k in (1, 2, 3)]
    + [("S", "x", k) for k in (1, 2, 3)]
    + [("S", "c")]
    + [("C", g, j) for g in range(GROUPS) for j in range(4)]
    + [("F", g, j) for g in range(GROUPS) for j in range(2)]
    + [("G", g, j, part) for g in range(GROUPS) for j in range(2) for part in range(2)]
    + [("Z", g, k) for g in range(GROUPS) for k in (1, 2, 3)]
)
COPY_ID = {name: index for index, name in enumerate(COPIES)}


def kernel(
    sections,
    features,
    act,
    grad,
    gain,
    preempted,
    weight,
    next_out,
    shadow_out,
    input_grad_out,
    gain_grad_out,
    weight_grad_out,
    act_v,
    grad_v,
    gain_v,
    preempted_v,
    wv,
    wp,
    xs,
    xs2,
    gains,
    got1,
    got2,
    acc,
    squares,
    outgoing,
    returned,
    partial,
    from_sib,
    hop,
    g_in,
    h_out,
    z_in,
    s_own,
    s_z,
    s_x,
    s_xr,
    s_c,
    s_cr,
    sums_s,
    mean_s,
    inv_s,
    dpre_s,
    dpre_t,
    send_sem,
    recv_sem,
    w_sem,
    in_sem,
):
    T, F = act.shape[1], act.shape[2]
    C = 4 * F
    count = [SPLIT[0], T - SPLIT[0]]
    start = [0, SPLIT[0]]
    rows = [slice(start[g], start[g] + count[g]) for g in range(GROUPS)]
    folded = [n + n // 2 for n in count]
    section, dp, z = lax.axis_index("section"), lax.axis_index("dp"), lax.axis_index("mp")
    core = dp % 2
    sib = dp + 1 - 2 * core
    odd = (z % 2) == 1

    def near(c, step):
        return (c + 2 * step + 8) % 8

    up, down, far = near(dp, 1), near(dp, -1), near(dp, 2)
    to_up, to_down, to_far, to_sib = {"dp": up}, {"dp": down}, {"dp": far}, {"dp": sib}
    to_next = {"section": (section + 1) % sections}
    to_back = {"section": (section + sections - 1) % sections}

    def to_z(k):
        return {"mp": (z + k) % 4}

    def zk(k):
        return (z + 4 - k) % 4

    def rc(name, src, dst, device):
        n = COPY_ID[name]
        return pltpu.make_async_remote_copy(
            src_ref=src,
            dst_ref=dst,
            send_sem=send_sem.at[n],
            recv_sem=recv_sem.at[n],
            device_id=device,
            device_id_type=MESH,
        )

    def send(name, src, dst, device):
        rc(name, src, dst, device).start()

    def arrive(name, dst):
        rc(name, dst, dst, to_sib).wait_recv()

    def sent(name, src):
        rc(name, src, src, to_sib).wait_send()

    small = [
        pltpu.make_async_copy(src, dst, in_sem.at[n])
        for n, (src, dst) in enumerate(
            ((act, act_v), (gain, gain_v), (grad, grad_v), (preempted, preempted_v))
        )
    ]

    def weight_copy(c):
        return pltpu.make_async_copy(weight.at[0, :, pl.ds(c * C, C)], wv.at[c], w_sem.at[c])

    for copy in small:
        copy.start()
    barrier = pltpu.get_barrier_semaphore()
    partners = [to_z(1), to_z(2), to_z(3), to_up, to_down, to_far, to_sib, to_next, to_back]
    for device in partners:
        pl.semaphore_signal(barrier, inc=1, device_id=device, device_id_type=MESH)
    for c in range(8):
        weight_copy(c).start()

    small[0].wait()
    small[1].wait()
    x_own = act_v[0].astype(F32)

    def put(block, g, value):
        main, fold = pack(value, odd)
        block[: count[g]] = main.astype(BF16)
        block[count[g] : folded[g]] = fold.astype(BF16)

    for g in range(GROUPS):
        put(got1[g].at[dp, z], g, x_own[rows[g]])
    gain_row = gain_v[...].astype(F32)
    g_main, g_rest = main_and_rest(jnp.broadcast_to(gain_row, (PAD, F)), odd)
    first_row = lax.broadcasted_iota(jnp.int32, (PAD, LANES), 0) == 0
    got1[0][dp, z, folded[0] :] = jnp.where(first_row, g_main, g_rest).astype(BF16)
    pl.semaphore_wait(barrier, len(partners))

    def own_to_z(tag, g, got):
        own = got.at[dp, z]
        for k in (1, 2, 3):
            send((tag, g, "z", k), own, own, to_z(k))

    def own_to_x(tag, g, got):
        own = got.at[dp, z]
        send((tag, g, "+", 0), own, own, to_up)
        send((tag, g, "-", 0), own, own, to_down)
        if tag == "a":
            send((tag, g, "f", 0), own, own, to_far)

    def from_z(tag, g, got, k):
        block = got.at[dp, zk(k)]
        arrive((tag, g, "z", k), block)
        send((tag, g, "+", k), block, block, to_up)
        send((tag, g, "-", k), block, block, to_down)
        if k == 3:
            send((tag, g, "f", 3), block, block, to_far)
            send((tag, g, "s", 0), got.at[dp], got.at[dp], to_sib)

    def from_x(tag, g, got, k):
        a, b = got.at[down, zk(k)], got.at[up, zk(k)]
        arrive((tag, g, "+", k), a)
        arrive((tag, g, "-", k), b)
        if k == 3:
            send((tag, g, "s", 1), got.at[down], got.at[down], to_sib)
            send((tag, g, "s", 2), got.at[up], got.at[up], to_sib)
        elif tag == "a" and k == 0:
            pass
        elif (k + g) % 2 == 0:
            send((tag, g, "f", k), a, a, to_up)
        else:
            send((tag, g, "f", k), b, b, to_down)

    def from_far(tag, g, got):
        for k in range(4):
            arrive((tag, g, "f", k), got.at[far, zk(k)])
        send((tag, g, "s", 3), got.at[far], got.at[far], to_sib)

    def from_sib_core(tag, g, got, j):
        arrive((tag, g, "s", j), got.at[near(sib, (0, -1, 1, 2)[j])])

    def gather_end(tag, g, got):
        for k in range(4):
            if k:
                sent((tag, g, "z", k), got.at[0, 0])
            for kind in "+-f":
                sent((tag, g, kind, k), got.at[0, 0])
            sent((tag, g, "s", k), got.at[0])

    def chunk_of(i):
        step = jnp.where(i < 2, 0, jnp.where(i > 5, 2, jnp.where(i % 2 == 0, 3, 1)))
        flip = jnp.where((i == 1) | (i == 4) | (i == 5) | (i == 7), 1, 0)
        mine = (dp + 2 * step) % 8
        return mine + flip * (1 - 2 * core)

    def steps(work, events):
        def body(i, carry):
            for n in sorted(events):

                @pl.when(i == n)
                def _():
                    for action, *arguments in events[n]:
                        action(*arguments)

            work(i)
            return carry

        lax.fori_loop(0, 8, body, 0)

    def gather_events(tag, got, extra):
        def z(g, k):
            return (from_z, tag, g, got[g], k)

        def x(g, k):
            return (from_x, tag, g, got[g], k)

        def s(g, j):
            return (from_sib_core, tag, g, got[g], j)

        def f(g):
            return (from_far, tag, g, got[g])

        first = {
            0: [z(0, 1), (own_to_z, tag, 1, got[1]), x(0, 0), z(0, 2), z(0, 3)],
            1: [x(0, 1), z(1, 1), s(0, 0)],
            2: [x(0, 2), z(1, 2), x(1, 0), x(0, 3), z(1, 3)],
            4: [x(1, 1), s(0, 1)],
            5: [x(1, 2), s(0, 2)],
            6: [f(0)],
            7: [x(1, 3), s(0, 3)],
        }
        second = {
            1: [s(1, 0)],
            4: [s(1, 1)],
            5: [s(1, 2)],
            6: [f(1)],
            7: [s(1, 3)],
        }
        for (g, n), actions in extra.items():
            events = (first, second)[g]
            events[n] = events.get(n, []) + actions
        return first, second

    own_to_z("a", 0, got1[0])
    for g in range(GROUPS):
        own_to_x("a", g, got1[g])

    ones = jnp.ones((PAD, C), BF16)

    def fill(c, carry):
        xs[c, :PAD] = ones
        wp[c, F:] = ones
        return carry

    lax.fori_loop(0, 8, fill, 0)

    low = [low_lanes(n // 2) for n in count]

    def unfold_chunk(got, g, c, keep):
        n, m = count[g], folded[g]
        total = squares[rows[g]]
        for p in range(2):
            r0 = got[c, 2 * p, n:m].astype(F32)
            r1 = got[c, 2 * p + 1, n:m].astype(F32)
            middle = jnp.concatenate(
                [jnp.where(low[g], r0, r1), half_turn(jnp.where(low[g], r1, r0))], axis=0
            )
            t0 = got[c, 2 * p, :n]
            t2 = got[c, 2 * p + 1, :n]
            keep(3 * p, t0)
            keep(3 * p + 1, middle.astype(BF16))
            keep(3 * p + 2, t2)
            t0, t2 = t0.astype(F32), t2.astype(F32)
            total = total + (t0 * t0 + middle * middle + t2 * t2)
        squares[rows[g]] = total

    spot = [slice(PAD + start[g], PAD + start[g] + count[g]) for g in range(GROUPS)]
    fed = [slice(0, PAD + count[0]), spot[1]]

    def first_layer(g):
        def work(i):
            c = chunk_of(i)
            if g == 0:
                row_low = low_lanes(1)
                for p in range(2):
                    g0 = got1[0][c, 2 * p, folded[0] :].astype(F32)
                    g1 = got1[0][c, 2 * p + 1, folded[0] :].astype(F32)
                    for j, row in enumerate((g0[0:1], jnp.where(row_low, g0[1:2], g1[1:2]), g1[0:1])):
                        gains[c, :, (3 * p + j) * LANES : (3 * p + j + 1) * LANES] = jnp.broadcast_to(
                            row, (8, LANES)
                        )
                wp[c, :F] = (wv[c].astype(F32) * gains[c, 0:1]).astype(BF16)

            def keep(t, value):
                xs[c, spot[g], t * LANES : (t + 1) * LANES] = value

            unfold_chunk(got1[g], g, c, keep)
            acc[fed[g]] += dot(xs[c, fed[g]], wp[c], NT)

        return work

    def second_layer(g):
        def work(i):
            c = chunk_of(i)

            def keep(t, value):
                xs2[: count[g], t * LANES : (t + 1) * LANES] = value

            unfold_chunk(got2[g], g, c, keep)
            acc[spot[g]] += dot(xs2[: count[g]], wp[c], NT)

        return work

    def row_statistics(g):
        mean = acc[spot[g], F : F + 1] / features
        variance = jnp.sum(squares[rows[g]], axis=1, keepdims=True) / features - mean * mean
        return mean, lax.rsqrt(variance + EPS)

    width = s_own.shape[1]
    row_is_0 = lax.broadcasted_iota(jnp.int32, (8, width), 0) == 0

    def finish_first(g):
        mean, inv_std = row_statistics(g)
        if g == 0:
            sums_s[...] = acc[0:8, :F]
        weight_sums = sums_s[0:1]
        preact = inv_std * (acc[spot[g], :F] - mean * weight_sums)
        t, slope = gelu_parts(preact)
        x = act_v[0, rows[g]].astype(F32)
        layer_out = x + 0.5 * preact * (1.0 + t)
        put(outgoing[g], g, layer_out.astype(BF16).astype(F32))
        send(("next", g), outgoing[g], got2[g].at[dp, z], to_next)

        derivative = 0.5 * (1.0 + t) + 0.5 * preact * (1.0 - t * t) * slope
        dpre = (grad_v[0, rows[g]].astype(F32) * derivative).astype(BF16)
        dpre_s[rows[g]] = dpre
        dpre_f = dpre.astype(F32)
        mean_s[rows[g]] = jnp.broadcast_to(mean, (count[g], LANES))
        inv_s[rows[g]] = jnp.broadcast_to(inv_std, (count[g], LANES))
        sum_grad = as_row(jnp.sum(dpre_f * weight_sums, axis=1, keepdims=True), width, start[g])
        sum_proj = as_row(jnp.sum(dpre_f * preact, axis=1, keepdims=True), width, start[g])
        both = jnp.where(row_is_0, sum_grad, sum_proj)
        s_own[...] = both if g == 0 else s_own[...] + both

    def finish_second(g):
        mean, inv_std = row_statistics(g)
        preact = inv_std * (acc[spot[g], :F] - mean * sums_s[0:1])
        t, _ = gelu_parts(preact)
        own = got2[g].at[dp, z]
        x = unpack(own[: count[g]].astype(F32), own[count[g] :].astype(F32), odd)
        redundant = (x + 0.5 * preact * (1.0 + t)).astype(BF16).astype(F32)
        sent(("next", g), outgoing[g])
        put(outgoing[g], g, redundant)
        send(("back", g), outgoing[g], returned[g], to_back)
        next_out[0, rows[g]] = jnp.where(section > 0, x, 0.0).astype(BF16)

    def x_of(j):
        return (dp // 2 + jnp.where(j == 0, 2, jnp.where(j == 1, 1, jnp.where(j == 2, 3, 0)))) % 4

    def partial_sums(g):
        n, h = count[g], count[g] // 2

        def body(i, carry):
            j = i % 4
            theirs = i < 4
            x = x_of(j)
            c = 2 * x + jnp.where(theirs, 1 - core, core)
            product = dot(dpre_s[rows[g]], wv[c], NN)
            for p in range(2):
                tile = [product[:, (3 * p + q) * LANES : (3 * p + q + 1) * LANES] for q in range(3)]
                top, bottom = tile[1][:h], half_turn(tile[1][h:])
                partial[g][c, 2 * p, :n] = tile[0].astype(BF16)
                partial[g][c, 2 * p, n:] = jnp.where(low[g], top, bottom).astype(BF16)
                partial[g][c, 2 * p + 1, :n] = tile[2].astype(BF16)
                partial[g][c, 2 * p + 1, n:] = jnp.where(low[g], bottom, top).astype(BF16)
            for m in range(4):

                @pl.when(i == m)
                def _():
                    send(("C", g, m), partial[g].at[c], from_sib[g].at[x], to_sib)

            return carry

        lax.fori_loop(0, 8, body, 0)

    def fold_in(g, c, source, index, first, blocks):
        for b in range(blocks):
            partial[g][c, first + b] = (
                partial[g][c, first + b].astype(F32) + source[index, b].astype(F32)
            ).astype(BF16)

    def from_sibling(g, n):
        x = x_of(n)
        arrive(("C", g, n), from_sib[g].at[x])
        fold_in(g, 2 * x + core, from_sib[g], x, 0, 4)

    def reduce_begin(g):
        from_sibling(g, 0)
        send(("F", g, 0), partial[g].at[far, 0:2], hop[g].at[0], to_up)
        send(("F", g, 1), partial[g].at[far, 2:4], hop[g].at[1], to_down)
        from_sibling(g, 1)
        send(("G", g, 0, 0), partial[g].at[up, 2:4], g_in[g].at[0, 2:4], to_up)
        from_sibling(g, 2)
        send(("G", g, 1, 0), partial[g].at[down, 0:2], g_in[g].at[1, 0:2], to_down)
        from_sibling(g, 3)

    def reduce_hop(g):
        arrive(("F", g, 0), hop[g].at[0])
        fold_in(g, up, hop[g], 0, 0, 2)
        send(("G", g, 0, 1), partial[g].at[up, 0:2], g_in[g].at[0, 0:2], to_up)
        arrive(("F", g, 1), hop[g].at[1])
        fold_in(g, down, hop[g], 1, 2, 2)
        send(("G", g, 1, 1), partial[g].at[down, 2:4], g_in[g].at[1, 2:4], to_down)

    def sum_x(g, b):
        return partial[g][dp, b].astype(F32) + (g_in[g][0, b].astype(F32) + g_in[g][1, b].astype(F32))

    def reduce_z(g):
        arrive(("G", g, 0, 0), g_in[g].at[0, 2:4])
        arrive(("G", g, 1, 0), g_in[g].at[1, 0:2])
        arrive(("G", g, 0, 1), g_in[g].at[0, 0:2])
        arrive(("G", g, 1, 1), g_in[g].at[1, 2:4])
        for k in (1, 2, 3):
            h_out[g][k - 1] = sum_x(g, (z + k) % 4).astype(BF16)
            send(("Z", g, k), h_out[g].at[k - 1], z_in[g].at[k - 1], to_z(k))

    def reduce_end(g):
        total = sum_x(g, z)
        for k in (1, 2, 3):
            arrive(("Z", g, k), z_in[g].at[k - 1])
            total = total + z_in[g][k - 1].astype(F32)
        return unpack(total[: count[g]], total[count[g] :], odd)

    def sums_x():
        for k in (1, 2, 3):
            arrive(("S", "z", k), s_z.at[k - 1])
        s_x[...] = s_own[...] + (s_z[0] + s_z[1] + s_z[2])
        for k in (1, 2, 3):
            send(("S", "x", k), s_x, s_xr.at[k - 1], {"dp": near(dp, k)})

    def sums_core():
        for k in (1, 2, 3):
            arrive(("S", "x", k), s_xr.at[k - 1])
        s_c[...] = s_x[...] + (s_xr[0] + s_xr[1] + s_xr[2])
        send(("S", "c"), s_c, s_cr, to_sib)

    def weight_grad_chunk(c, carry):
        x = xs[c, PAD:].astype(F32)
        normed = ((x - mean_s[:, 0:1]) * inv_s[:, 0:1] * gains[c, 0:1]).astype(BF16)
        weight_grad_out[0, :, pl.ds(pl.multiple_of(c * C, C), C)] = dot(dpre_t[...], normed, NN).astype(BF16)
        return carry

    acc[...] = jnp.zeros_like(acc)
    squares[...] = jnp.zeros_like(squares)
    for c in range(8):
        weight_copy(c).wait()
    small[2].wait()
    small[3].wait()
    events = gather_events("a", got1, {(1, 1): [(reduce_begin, 0)]})
    steps(first_layer(0), events[0])
    finish_first(0)
    partial_sums(0)
    steps(first_layer(1), events[1])
    finish_first(1)
    for k in (1, 2, 3):
        send(("S", "z", k), s_own, s_z.at[k - 1], to_z(k))
    partial_sums(1)
    acc[...] = jnp.zeros_like(acc)
    squares[...] = jnp.zeros_like(squares)
    reduce_begin(1)

    arrive(("next", 0), got2[0].at[dp, z])
    own_to_z("b", 0, got2[0])
    own_to_x("b", 0, got2[0])
    dpre_t[...] = dot(jnp.where(eye(F, F), 1.0, 0.0).astype(BF16), dpre_s[...], NT).astype(BF16)
    lax.fori_loop(0, 6, weight_grad_chunk, 0)
    reduce_hop(0)
    arrive(("next", 1), got2[1].at[dp, z])
    own_to_x("b", 1, got2[1])
    sums_x()
    events = gather_events(
        "b",
        got2,
        {(0, 6): [(sums_core,)], (0, 7): [(reduce_hop, 1)]},
    )
    steps(second_layer(0), events[0])
    finish_second(0)
    lax.fori_loop(6, 8, weight_grad_chunk, 0)
    steps(second_layer(1), events[1])
    finish_second(1)
    for g in range(GROUPS):
        reduce_z(g)

    dnormed = jnp.concatenate([reduce_end(g) for g in range(GROUPS)], axis=0)
    arrive(("S", "c"), s_cr)
    sums = (s_c[...] + s_cr[...])[:, :T] / features
    mean_grad = as_column(sums[0:1])
    mean_proj = as_column(sums[1:2])
    inv_std = inv_s[:, 0:1]
    x_hat = (act_v[0].astype(F32) - mean_s[:, 0:1]) * inv_std
    gain_grad_out[...] = jnp.sum(dnormed * x_hat, axis=0, keepdims=True)
    dhat = dnormed * gain_v[...].astype(F32)
    dinput = inv_std * (dhat - mean_grad - x_hat * mean_proj)
    input_grad_out[0] = (grad_v[0].astype(F32) + dinput).astype(BF16)

    active = as_column(preempted_v[...].astype(F32)) * jnp.where(section < sections - 1, 1.0, 0.0)
    for g in range(GROUPS):
        arrive(("back", g), returned[g])
        shadow = unpack(returned[g][: count[g]].astype(F32), returned[g][count[g] :].astype(F32), odd)
        shadow_out[0, rows[g]] = (shadow * active[rows[g]]).astype(BF16)

    for k in (1, 2, 3):
        sent(("S", "z", k), s_own)
        sent(("S", "x", k), s_x)
    sent(("S", "c"), s_c)
    for g in range(GROUPS):
        gather_end("a", g, got1[g])
        gather_end("b", g, got2[g])
        sent(("back", g), outgoing[g])
        for k in (1, 2, 3):
            sent(("Z", g, k), h_out[g].at[k - 1])
        for n in range(4):
            sent(("C", g, n), partial[g].at[0])
        for j in range(2):
            sent(("F", g, j), hop[g].at[0])
            for part in range(2):
                sent(("G", g, j, part), hop[g].at[0])


def shards(sections, act_in, grad_in, weight, gain, preempted):
    _, T, F = act_in.shape
    D = weight.shape[2]
    C = 4 * F
    anywhere = pl.BlockSpec(memory_space=pl.ANY)
    shape = jax.ShapeDtypeStruct
    copies = len(COPIES)
    count = (SPLIT[0], T - SPLIT[0])
    folded = [n + n // 2 for n in count]
    results = (
        shape((1, T, F), BF16),
        shape((1, T, F), BF16),
        shape((1, T, F), BF16),
        shape((1, F), F32),
        shape((1, F, D), BF16),
    )

    def blocks(*lead, extra=(0, 0)):
        return tuple(pltpu.VMEM((*lead, m + e, LANES), BF16) for m, e in zip(folded, extra))

    results = pl.pallas_call(
        functools.partial(kernel, sections, float(D)),
        out_shape=results,
        in_specs=[anywhere] * 5,
        out_specs=(pl.BlockSpec(memory_space=pltpu.VMEM),) * 5,
        scratch_shapes=[
            pltpu.VMEM((1, T, F), BF16),
            pltpu.VMEM((1, T, F), BF16),
            pltpu.VMEM((1, F), BF16),
            pltpu.VMEM((1, T), jnp.int32),
            pltpu.VMEM((8, F, C), BF16),
            pltpu.VMEM((8, F + PAD, C), BF16),
            pltpu.VMEM((8, PAD + T, C), BF16),
            pltpu.VMEM((max(count), C), BF16),
            pltpu.VMEM((8, 8, C), F32),
            blocks(8, 4, extra=(PAD, 0)),
            blocks(8, 4),
            pltpu.VMEM((PAD + T, F + PAD), F32),
            pltpu.VMEM((T, LANES), F32),
            blocks(),
            blocks(),
            blocks(8, 4),
            blocks(4, 4),
            blocks(2, 2),
            blocks(2, 4),
            blocks(3),
            blocks(3),
            pltpu.VMEM((8, 256), F32),
            pltpu.VMEM((3, 8, 256), F32),
            pltpu.VMEM((8, 256), F32),
            pltpu.VMEM((3, 8, 256), F32),
            pltpu.VMEM((8, 256), F32),
            pltpu.VMEM((8, 256), F32),
            pltpu.VMEM((8, F), F32),
            pltpu.VMEM((T, LANES), F32),
            pltpu.VMEM((T, LANES), F32),
            pltpu.VMEM((T, F), BF16),
            pltpu.VMEM((F, T), BF16),
            pltpu.SemaphoreType.DMA((copies,)),
            pltpu.SemaphoreType.DMA((copies,)),
            pltpu.SemaphoreType.DMA((8,)),
            pltpu.SemaphoreType.DMA((4,)),
        ],
        compiler_params=pltpu.CompilerParams(
            collective_id=0, has_side_effects=True, vmem_limit_bytes=48 * 1024 * 1024
        ),
    )(*[pltpu.with_memory_space_constraint(a, pltpu.HBM) for a in (act_in, grad_in, gain, preempted, weight)])
    next_input, shadow, input_grad, gain_grad, weight_grad = results
    return next_input, shadow, input_grad, weight_grad, gain_grad


def solution(mesh):
    return jax.shard_map(
        functools.partial(shards, mesh.shape["section"]),
        mesh=mesh,
        in_specs=(
            P("section", None, ("dp", "mp")),
            P("section", None, ("dp", "mp")),
            P("section", ("dp", "mp"), None),
            P("section", ("dp", "mp")),
            P("section", None),
        ),
        out_specs=(
            P("section", None, ("dp", "mp")),
            P("section", None, ("dp", "mp")),
            P("section", None, ("dp", "mp")),
            P("section", ("dp", "mp"), None),
            P("section", ("dp", "mp")),
        ),
        check_vma=False,
    )
```

time: 714 us -> 74.4 us (0.10); the launches traced: 701 us -> 74.2 us
  waiting for transfers between devices: 493 us -> 0 us
  blocking collectives: 141 us -> 0 us
  Pallas kernels: 0 us -> 69.7 us
  local copies, waits for them, and re-layouts: 24 us -> 3.87 us
  between operations: 13.9 us -> 0.64 us
  matrix products: 11.6 us -> 0 us
  starting transfers between devices: 10.6 us -> 0 us
    all_gather x2 -> x0, waiting for transfers between devices: 324 us -> none  [layer_forward(): gathered = lax.all_gather(normed, ('dp', 'mp'), axis=1, tiled=True)]
    unnamed x4 -> x0, waiting for transfers between devices: 161 us -> none
    psum x2 -> x0, blocking collectives: 141 us -> none  [row_totals(): return lax.psum((pieces[0], pieces[1]), ('dp', 'mp'))]
    pallas_call x0 -> x1, Pallas kernels: none -> 69.7 us  [shards(): pl.pallas_call(functools.partial(kernel, sections, float(D)), out_shape=r...]
    unnamed x13 -> x5, local copies, waits for them, and re-layouts: 16.1 us -> 3.87 us
    dot_general x4 -> x0, matrix products: 11.6 us -> none  [the longest x2 6.56 us: layer_forward(): lax.dot_general(gathered, weights, (((1,), (1,)), ((), ())), preferred_el...]
    ppermute x3 -> x0, starting transfers between devices: 10.5 us -> none  [passed_along(): lax.ppermute(value, axis, [(source, source + steps) for source in range(i...]
    ppermute x3 -> x0, waiting for transfers between devices: 8 us -> none  [passed_along(): lax.ppermute(value, axis, [(source, source + steps) for source in range(i...]
  transfers between devices with their start and end apart: 6 -> 0, of which waited for: 5 -> 0; matrix products, arithmetic and copies ran while one was open for 1% -> 0% of each run, Pallas kernels for 0% -> 0%
where the time goes in v2:
time: 74.4 us; the launch traced here: 74.2 us
  Pallas kernels  69.7 us (94%)
  local copies, waits for them, and re-layouts  3.87 us (5%)
    pallas_call x1, Pallas kernels, shards(): pl.pallas_call(functools.partial(kernel, sections, float(D)), out_shape=r...  69.7 us
    unnamed x5, local copies, waits for them, and re-layouts  3.87 us

profile of v2, /device:TPU:1, one launch (start us, length us, event | category | flops | bytes accessed | tf_op | source)
XLA Modules:
  0.0 74.2 jit_solution(7180109052684004053)
XLA Ops:
  0.6 69.7 %shard_map.92 = (bf16[1,160,192]{2,1,0:T(8,128)(2,1)S(1)}, bf16[1,160,192]{2,1,0:T(8,128)(2,1)S(1)}, bf16[1,160,192]{2,1,0:T(8,128)(2,1)S(1)}, f32[1,192]{1,0:T(1,128)S(1)}, bf16[1,192,6144]{2,1,0:T(8,128)(2,1)S(1)}) custom-call(bf16[1,160,192]{2,1,0:T(8,128)(2,1)} %act.1, bf16[1,160,192]{2,1,0:T(8,128)(2,1)} %grad.1, bf16[1,192]{1,0:T(2,128)(2,1)} %gain.1, ...), custom_call_target="tpu_custom_call" | custom-call | tf_op jit(solution)/shard_map/pallas_call | solution.py:649
  70.3 0.6 copy.15
  71.0 0.6 copy.16
  71.6 0.6 copy.17
  72.2 1.4 %copy.18 = bf16[1,192,6144]{2,1,0:T(8,128)(2,1)} copy(bf16[1,192,6144]{2,1,0:T(8,128)(2,1)S(1)} %get-tuple-element.23) | data formatting | bytes 4718592
  73.6 0.6 copy.19

commit v3 on v2

--- a/solution.py
+++ b/solution.py
@@ -88,6 +88,7 @@
 
 GROUPS = 2
 SPLIT = (96, 64)
+DIRECT = {"a": (0, 3), "b": (3,)}
 COPIES = (
     [(tag, g, "z", k) for tag in "ab" for g in range(GROUPS) for k in (1, 2, 3)]
     + [(tag, g, kind, k) for tag in "ab" for g in range(GROUPS) for kind in "+-s" for k in range(4)]
@@ -112,9 +113,7 @@
     gain,
     preempted,
     weight,
-    next_out,
-    shadow_out,
-    input_grad_out,
+    rows_out,
     gain_grad_out,
     weight_grad_out,
     act_v,
@@ -149,6 +148,8 @@
     inv_s,
     dpre_s,
     dpre_t,
+    held,
+    hat_s,
     send_sem,
     recv_sem,
     w_sem,
@@ -176,11 +177,20 @@
     def to_z(k):
         return {"mp": (z + k) % 4}
 
+    def nth(k):
+        if k == 1:
+            return jnp.where(z % 2 == 0, 3, 1)
+        if k == 2:
+            return jnp.where(z == 1, 3, jnp.where(z == 2, 1, 2))
+        if k == 3:
+            return jnp.where(z == 0, 1, jnp.where(z == 3, 3, 2))
+        return 0
+
     def zk(k):
-        return (z + 4 - k) % 4
-
-    def rc(name, src, dst, device):
-        n = COPY_ID[name]
+        return (z + 4 - nth(k)) % 4
+
+    def rc(name, src, dst, device, offset=0):
+        n = COPY_ID[name] + offset
         return pltpu.make_async_remote_copy(
             src_ref=src,
             dst_ref=dst,
@@ -193,8 +203,8 @@
     def send(name, src, dst, device):
         rc(name, src, dst, device).start()
 
-    def arrive(name, dst):
-        rc(name, dst, dst, to_sib).wait_recv()
+    def arrive(name, dst, offset=0):
+        rc(name, dst, dst, to_sib, offset).wait_recv()
 
     def sent(name, src):
         rc(name, src, src, to_sib).wait_send()
@@ -244,16 +254,17 @@
         own = got.at[dp, z]
         send((tag, g, "+", 0), own, own, to_up)
         send((tag, g, "-", 0), own, own, to_down)
-        if tag == "a":
+        if 0 in DIRECT[tag]:
             send((tag, g, "f", 0), own, own, to_far)
 
     def from_z(tag, g, got, k):
         block = got.at[dp, zk(k)]
-        arrive((tag, g, "z", k), block)
+        arrive((tag, g, "z", 1), block, nth(k) - 1)
         send((tag, g, "+", k), block, block, to_up)
         send((tag, g, "-", k), block, block, to_down)
+        if k in DIRECT[tag]:
+            send((tag, g, "f", k), block, block, to_far)
         if k == 3:
-            send((tag, g, "f", 3), block, block, to_far)
             send((tag, g, "s", 0), got.at[dp], got.at[dp], to_sib)
 
     def from_x(tag, g, got, k):
@@ -263,7 +274,7 @@
         if k == 3:
             send((tag, g, "s", 1), got.at[down], got.at[down], to_sib)
             send((tag, g, "s", 2), got.at[up], got.at[up], to_sib)
-        elif tag == "a" and k == 0:
+        if k in DIRECT[tag]:
             pass
         elif (k + g) % 2 == 0:
             send((tag, g, "f", k), a, a, to_up)
@@ -326,13 +337,14 @@
             4: [x(1, 1), s(0, 1)],
             5: [x(1, 2), s(0, 2)],
             6: [f(0)],
-            7: [x(1, 3), s(0, 3)],
+            7: [s(0, 3)],
         }
         second = {
+            0: [x(1, 3)],
             1: [s(1, 0)],
+            3: [f(1)],
             4: [s(1, 1)],
             5: [s(1, 2)],
-            6: [f(1)],
             7: [s(1, 3)],
         }
         for (g, n), actions in extra.items():
@@ -451,7 +463,7 @@
         sent(("next", g), outgoing[g])
         put(outgoing[g], g, redundant)
         send(("back", g), outgoing[g], returned[g], to_back)
-        next_out[0, rows[g]] = jnp.where(section > 0, x, 0.0).astype(BF16)
+        rows_out[0, rows[g]] = jnp.where(section > 0, x, 0.0).astype(BF16)
 
     def x_of(j):
         return (dp // 2 + jnp.where(j == 0, 2, jnp.where(j == 1, 1, jnp.where(j == 2, 3, 0)))) % 4
@@ -555,7 +567,7 @@
         weight_copy(c).wait()
     small[2].wait()
     small[3].wait()
-    events = gather_events("a", got1, {(1, 1): [(reduce_begin, 0)]})
+    events = gather_events("a", got1, {(1, 2): [(reduce_begin, 0)]})
     steps(first_layer(0), events[0])
     finish_first(0)
     partial_sums(0)
@@ -572,41 +584,43 @@
     own_to_z("b", 0, got2[0])
     own_to_x("b", 0, got2[0])
     dpre_t[...] = dot(jnp.where(eye(F, F), 1.0, 0.0).astype(BF16), dpre_s[...], NT).astype(BF16)
-    lax.fori_loop(0, 6, weight_grad_chunk, 0)
     reduce_hop(0)
+    lax.fori_loop(0, 8, weight_grad_chunk, 0)
     arrive(("next", 1), got2[1].at[dp, z])
     own_to_x("b", 1, got2[1])
+    reduce_hop(1)
     sums_x()
     events = gather_events(
         "b",
         got2,
-        {(0, 6): [(sums_core,)], (0, 7): [(reduce_hop, 1)]},
+        {(0, 1): [(reduce_z, 0)], (1, 0): [(reduce_z, 1)], (1, 4): [(sums_core,)]},
     )
     steps(second_layer(0), events[0])
     finish_second(0)
-    lax.fori_loop(6, 8, weight_grad_chunk, 0)
     steps(second_layer(1), events[1])
     finish_second(1)
-    for g in range(GROUPS):
-        reduce_z(g)
-
-    dnormed = jnp.concatenate([reduce_end(g) for g in range(GROUPS)], axis=0)
+
+    active = as_column(preempted_v[...].astype(F32)) * jnp.where(section < sections - 1, 1.0, 0.0)
     arrive(("S", "c"), s_cr)
     sums = (s_c[...] + s_cr[...])[:, :T] / features
     mean_grad = as_column(sums[0:1])
     mean_proj = as_column(sums[1:2])
     inv_std = inv_s[:, 0:1]
     x_hat = (act_v[0].astype(F32) - mean_s[:, 0:1]) * inv_std
-    gain_grad_out[...] = jnp.sum(dnormed * x_hat, axis=0, keepdims=True)
-    dhat = dnormed * gain_v[...].astype(F32)
-    dinput = inv_std * (dhat - mean_grad - x_hat * mean_proj)
-    input_grad_out[0] = (grad_v[0].astype(F32) + dinput).astype(BF16)
-
-    active = as_column(preempted_v[...].astype(F32)) * jnp.where(section < sections - 1, 1.0, 0.0)
+    held[...] = grad_v[0].astype(F32) - inv_std * (mean_grad + x_hat * mean_proj)
+    hat_s[...] = x_hat
+    gain_grad = jnp.zeros((1, F), F32)
+    for g in range(GROUPS):
+        dnormed = reduce_end(g)
+        gain_grad = gain_grad + jnp.sum(dnormed * hat_s[rows[g]], axis=0, keepdims=True)
+        dhat = dnormed * gain_v[...].astype(F32)
+        rows_out[2, rows[g]] = (held[rows[g]] + inv_s[rows[g], 0:1] * dhat).astype(BF16)
+    gain_grad_out[...] = gain_grad
+
     for g in range(GROUPS):
         arrive(("back", g), returned[g])
         shadow = unpack(returned[g][: count[g]].astype(F32), returned[g][count[g] :].astype(F32), odd)
-        shadow_out[0, rows[g]] = (shadow * active[rows[g]]).astype(BF16)
+        rows_out[1, rows[g]] = (shadow * active[rows[g]]).astype(BF16)
 
     for k in (1, 2, 3):
         sent(("S", "z", k), s_own)
@@ -636,9 +650,7 @@
     count = (SPLIT[0], T - SPLIT[0])
     folded = [n + n // 2 for n in count]
     results = (
-        shape((1, T, F), BF16),
-        shape((1, T, F), BF16),
-        shape((1, T, F), BF16),
+        shape((3, T, F), BF16),
         shape((1, F), F32),
         shape((1, F, D), BF16),
     )
@@ -650,7 +662,7 @@
         functools.partial(kernel, sections, float(D)),
         out_shape=results,
         in_specs=[anywhere] * 5,
-        out_specs=(pl.BlockSpec(memory_space=pltpu.VMEM),) * 5,
+        out_specs=(pl.BlockSpec(memory_space=pltpu.VMEM),) * 3,
         scratch_shapes=[
             pltpu.VMEM((1, T, F), BF16),
             pltpu.VMEM((1, T, F), BF16),
@@ -684,6 +696,8 @@
             pltpu.VMEM((T, LANES), F32),
             pltpu.VMEM((T, F), BF16),
             pltpu.VMEM((F, T), BF16),
+            pltpu.VMEM((T, F), F32),
+            pltpu.VMEM((T, F), F32),
             pltpu.SemaphoreType.DMA((copies,)),
             pltpu.SemaphoreType.DMA((copies,)),
             pltpu.SemaphoreType.DMA((8,)),
@@ -693,7 +707,8 @@
             collective_id=0, has_side_effects=True, vmem_limit_bytes=48 * 1024 * 1024
         ),
     )(*[pltpu.with_memory_space_constraint(a, pltpu.HBM) for a in (act_in, grad_in, gain, preempted, weight)])
-    next_input, shadow, input_grad, gain_grad, weight_grad = results
+    by_row, gain_grad, weight_grad = results
+    next_input, shadow, input_grad = by_row[0:1], by_row[1:2], by_row[2:3]
     return next_input, shadow, input_grad, weight_grad, gain_grad
 
 

time: 74.4 us -> 69.6 us (0.935)
  Pallas kernels: 69.7 us -> 66.2 us
  local copies, waits for them, and re-layouts: 3.87 us -> 2.66 us
    pallas_call x1, Pallas kernels: 69.7 us -> 66.2 us  [shards(): pl.pallas_call(functools.partial(kernel, sections, float(D)), out_shape=r...]
    unnamed x5 -> x2, local copies, waits for them, and re-layouts: 3.87 us -> 1.97 us
where the time goes in v3:
time: 69.6 us; the launch traced here: 69.5 us
  Pallas kernels  66.2 us (95%)
  local copies, waits for them, and re-layouts  2.66 us (4%)
    pallas_call x1, Pallas kernels, shards(): pl.pallas_call(functools.partial(kernel, sections, float(D)), out_shape=r...  66.2 us
    unnamed x2, local copies, waits for them, and re-layouts  1.97 us

profile of v3, /device:TPU:1, one launch (start us, length us, event | category | flops | bytes accessed | tf_op | source)
XLA Modules:
  0.0 69.5 jit_solution(13416053662146721679)
XLA Ops:
  0.6 66.2 %shard_map.92 = (bf16[3,160,192]{2,1,0:T(8,128)(2,1)S(1)}, f32[1,192]{1,0:T(1,128)S(1)}, bf16[1,192,6144]{2,1,0:T(8,128)(2,1)S(1)}) custom-call(bf16[1,160,192]{2,1,0:T(8,128)(2,1)} %act.1, bf16[1,160,192]{2,1,0:T(8,128)(2,1)} %grad.1, bf16[1,192]{1,0:T(2,128)(2,1)} %gain.1, s32[1,160]{1,0:T(1,128)} %preempted.1, bf16[1,192,6144]{2,1,0:T(8,128)(2,1)} %weight.1), custom_call_target="tpu_custom_call" | custom-call | tf_op jit(solution)/shard_map/pallas_call | solution.py:661
  66.8 0.7 %fusion = (bf16[1,160,192]{2,1,0:T(8,128)(2,1)}, bf16[1,160,192]{2,1,0:T(8,128)(2,1)}, bf16[1,160,192]{2,1,0:T(8,128)(2,1)}) fusion(bf16[3,160,192]{2,1,0:T(8,128)(2,1)S(1)} %get-tuple-element.8), kind=kLoop, calls=%fused_computation | loop fusion | bytes 368640 | tf_op jit(solution)/shard_map/slice | solution.py:711
  67.5 1.4 %copy.12 = bf16[1,192,6144]{2,1,0:T(8,128)(2,1)} copy(bf16[1,192,6144]{2,1,0:T(8,128)(2,1)S(1)} %get-tuple-element.22) | data formatting | bytes 4718592
  68.9 0.6 copy.13

commit v4 on v3

--- a/solution.py
+++ b/solution.py
@@ -91,8 +91,8 @@
 DIRECT = {"a": (0, 3), "b": (3,)}
 COPIES = (
     [(tag, g, "z", k) for tag in "ab" for g in range(GROUPS) for k in (1, 2, 3)]
-    + [(tag, g, kind, k) for tag in "ab" for g in range(GROUPS) for kind in "+-s" for k in range(4)]
-    + [(tag, g, "f", k) for tag in "ab" for g in range(GROUPS) for k in range(4)]
+    + [(tag, g, kind, k) for tag in "ab" for g in range(GROUPS) for kind in "+-s" for k in range(4) if (kind, k) != ("s", 3)]
+    + [(tag, g, kind, k) for tag in "ab" for g in range(GROUPS) for kind in "ft" for k in range(4)]
     + [(name, g) for name in ("next", "back") for g in range(GROUPS)]
     + [("S", "z", k) for k in (1, 2, 3)]
     + [("S", "x", k) for k in (1, 2, 3)]
@@ -219,12 +219,12 @@
     def weight_copy(c):
         return pltpu.make_async_copy(weight.at[0, :, pl.ds(c * C, C)], wv.at[c], w_sem.at[c])
 
-    for copy in small:
-        copy.start()
     barrier = pltpu.get_barrier_semaphore()
     partners = [to_z(1), to_z(2), to_z(3), to_up, to_down, to_far, to_sib, to_next, to_back]
     for device in partners:
         pl.semaphore_signal(barrier, inc=1, device_id=device, device_id_type=MESH)
+    for copy in small:
+        copy.start()
     for c in range(8):
         weight_copy(c).start()
 
@@ -269,25 +269,33 @@
 
     def from_x(tag, g, got, k):
         a, b = got.at[down, zk(k)], got.at[up, zk(k)]
-        arrive((tag, g, "+", k), a)
-        arrive((tag, g, "-", k), b)
+        if (k + g) % 2 == 0:
+            arrive((tag, g, "+", k), a)
+            if k not in DIRECT[tag]:
+                send((tag, g, "f", k), a, a, to_up)
+            arrive((tag, g, "-", k), b)
+        else:
+            arrive((tag, g, "-", k), b)
+            if k not in DIRECT[tag]:
+                send((tag, g, "f", k), b, b, to_down)
+            arrive((tag, g, "+", k), a)
         if k == 3:
             send((tag, g, "s", 1), got.at[down], got.at[down], to_sib)
             send((tag, g, "s", 2), got.at[up], got.at[up], to_sib)
-        if k in DIRECT[tag]:
-            pass
-        elif (k + g) % 2 == 0:
-            send((tag, g, "f", k), a, a, to_up)
-        else:
-            send((tag, g, "f", k), b, b, to_down)
 
     def from_far(tag, g, got):
         for k in range(4):
-            arrive((tag, g, "f", k), got.at[far, zk(k)])
-        send((tag, g, "s", 3), got.at[far], got.at[far], to_sib)
+            block = got.at[far, zk(k)]
+            arrive((tag, g, "f", k), block)
+            send((tag, g, "t", k), block, block, to_sib)
 
     def from_sib_core(tag, g, got, j):
-        arrive((tag, g, "s", j), got.at[near(sib, (0, -1, 1, 2)[j])])
+        c = near(sib, (0, -1, 1, 2)[j])
+        if j < 3:
+            arrive((tag, g, "s", j), got.at[c])
+        else:
+            for k in range(4):
+                arrive((tag, g, "t", k), got.at[c, zk(k)])
 
     def gather_end(tag, g, got):
         for k in range(4):
@@ -295,7 +303,9 @@
                 sent((tag, g, "z", k), got.at[0, 0])
             for kind in "+-f":
                 sent((tag, g, kind, k), got.at[0, 0])
-            sent((tag, g, "s", k), got.at[0])
+            sent((tag, g, "t", k), got.at[0, 0])
+            if k < 3:
+                sent((tag, g, "s", k), got.at[0])
 
     def chunk_of(i):
         step = jnp.where(i < 2, 0, jnp.where(i > 5, 2, jnp.where(i % 2 == 0, 3, 1)))
@@ -457,12 +467,15 @@
         mean, inv_std = row_statistics(g)
         preact = inv_std * (acc[spot[g], :F] - mean * sums_s[0:1])
         t, _ = gelu_parts(preact)
+        redundant = (hat_s[rows[g]] + 0.5 * preact * (1.0 + t)).astype(BF16).astype(F32)
+        put(outgoing[g], g, redundant)
+        send(("back", g), outgoing[g], returned[g], to_back)
+
+    def predecessor(g):
+        sent(("next", g), outgoing[g])
         own = got2[g].at[dp, z]
         x = unpack(own[: count[g]].astype(F32), own[count[g] :].astype(F32), odd)
-        redundant = (x + 0.5 * preact * (1.0 + t)).astype(BF16).astype(F32)
-        sent(("next", g), outgoing[g])
-        put(outgoing[g], g, redundant)
-        send(("back", g), outgoing[g], returned[g], to_back)
+        hat_s[rows[g]] = x
         rows_out[0, rows[g]] = jnp.where(section > 0, x, 0.0).astype(BF16)
 
     def x_of(j):
@@ -580,15 +593,19 @@
     squares[...] = jnp.zeros_like(squares)
     reduce_begin(1)
 
+    reduce_hop(0)
     arrive(("next", 0), got2[0].at[dp, z])
     own_to_z("b", 0, got2[0])
     own_to_x("b", 0, got2[0])
     dpre_t[...] = dot(jnp.where(eye(F, F), 1.0, 0.0).astype(BF16), dpre_s[...], NT).astype(BF16)
-    reduce_hop(0)
     lax.fori_loop(0, 8, weight_grad_chunk, 0)
+    for g in range(GROUPS):
+        gather_end("a", g, got1[g])
     arrive(("next", 1), got2[1].at[dp, z])
     own_to_x("b", 1, got2[1])
     reduce_hop(1)
+    for g in range(GROUPS):
+        predecessor(g)
     sums_x()
     events = gather_events(
         "b",
@@ -617,17 +634,11 @@
         rows_out[2, rows[g]] = (held[rows[g]] + inv_s[rows[g], 0:1] * dhat).astype(BF16)
     gain_grad_out[...] = gain_grad
 
-    for g in range(GROUPS):
-        arrive(("back", g), returned[g])
-        shadow = unpack(returned[g][: count[g]].astype(F32), returned[g][count[g] :].astype(F32), odd)
-        rows_out[1, rows[g]] = (shadow * active[rows[g]]).astype(BF16)
-
     for k in (1, 2, 3):
         sent(("S", "z", k), s_own)
         sent(("S", "x", k), s_x)
     sent(("S", "c"), s_c)
     for g in range(GROUPS):
-        gather_end("a", g, got1[g])
         gather_end("b", g, got2[g])
         sent(("back", g), outgoing[g])
         for k in (1, 2, 3):
@@ -638,6 +649,11 @@
             sent(("F", g, j), hop[g].at[0])
             for part in range(2):
                 sent(("G", g, j, part), hop[g].at[0])
+
+    for g in range(GROUPS):
+        arrive(("back", g), returned[g])
+        shadow = unpack(returned[g][: count[g]].astype(F32), returned[g][count[g] :].astype(F32), odd)
+        rows_out[1, rows[g]] = (shadow * active[rows[g]]).astype(BF16)
 
 
 def shards(sections, act_in, grad_in, weight, gain, preempted):

time: 69.6 us -> 69.4 us (level)
  no operation moved by 1% of the time
where the time goes in v4:
time: 69.4 us; the launch traced here: 69.3 us
  Pallas kernels  66 us (95%)
  local copies, waits for them, and re-layouts  2.66 us (4%)
    pallas_call x1, Pallas kernels, shards(): pl.pallas_call(functools.partial(kernel, sections, float(D)), out_shape=r...  66 us
    unnamed x2, local copies, waits for them, and re-layouts  1.97 us

profile of v4, /device:TPU:1, one launch (start us, length us, event | category | flops | bytes accessed | tf_op | source)
XLA Modules:
  0.0 69.3 jit_solution(10283711488265512208)
XLA Ops:
  0.6 66.0 %shard_map.92 = (bf16[3,160,192]{2,1,0:T(8,128)(2,1)S(1)}, f32[1,192]{1,0:T(1,128)S(1)}, bf16[1,192,6144]{2,1,0:T(8,128)(2,1)S(1)}) custom-call(bf16[1,160,192]{2,1,0:T(8,128)(2,1)} %act.1, bf16[1,160,192]{2,1,0:T(8,128)(2,1)} %grad.1, bf16[1,192]{1,0:T(2,128)(2,1)} %gain.1, s32[1,160]{1,0:T(1,128)} %preempted.1, bf16[1,192,6144]{2,1,0:T(8,128)(2,1)} %weight.1), custom_call_target="tpu_custom_call" | custom-call | tf_op jit(solution)/shard_map/pallas_call | solution.py:677
  66.6 0.7 %fusion = (bf16[1,160,192]{2,1,0:T(8,128)(2,1)}, bf16[1,160,192]{2,1,0:T(8,128)(2,1)}, bf16[1,160,192]{2,1,0:T(8,128)(2,1)}) fusion(bf16[3,160,192]{2,1,0:T(8,128)(2,1)S(1)} %get-tuple-element.8), kind=kLoop, calls=%fused_computation | loop fusion | bytes 368640 | tf_op jit(solution)/shard_map/slice | solution.py:727
  67.3 1.4 %copy.12 = bf16[1,192,6144]{2,1,0:T(8,128)(2,1)} copy(bf16[1,192,6144]{2,1,0:T(8,128)(2,1)S(1)} %get-tuple-element.22) | data formatting | bytes 4718592
  68.7 0.6 copy.13
